TPU v7x, 512 devices: a whole 4x4x16 slice. The times are simulated.
512 devices in a mesh: blk: 16 (over z), resp: 16 (over y_hi, x, core), head: 2 (over y_lo).
Axes of the slice: x: 4, y: 4 (y_hi: 2, y_lo: 2; y = y_hi * 2 + y_lo), z: 16, core: 2. Of those that a mesh axis runs over, the one named last changes fastest.
Arguments:
- queries: bfloat16 [65536, 4096], P(('blk', 'resp'), 'head'), may hold values from -6 to 6
- out_grad: bfloat16 [65536, 4096], P(('blk', 'resp'), 'head'), may hold values from -6 to 6
- prompt_keys: bfloat16 [2, 1024, 512], P(None, 'blk', 'head'), may hold values from -6 to 6
- prompt_values: bfloat16 [2, 1024, 512], P(None, 'blk', 'head'), may hold values from -6 to 6
- resp_prompt: int32 [256], P(('blk', 'resp')), may hold values from 0 to 1, as said below
- resp_len: int32 [256], P(('blk', 'resp')), may hold values from 128 to 256, as said below
Outputs:
- query_grad: bfloat16 [65536, 4096], P(('blk', 'resp'), 'head')
- prompt_key_grad: bfloat16 [2, 1024, 512], P(None, ('blk', 'resp'), 'head')
- prompt_value_grad: bfloat16 [2, 1024, 512], P(None, ('blk', 'resp'), 'head')
Inputs may be any that keep to these rules, and one draw needn't show every extreme that they name: `resp_prompt`: each of the 2 prompts is named by exactly 128 responses. `resp_len`: multiples of 128; some response has 256 and some has 128.
All inputs are finite; a program needn't handle non-finite values.
Results may differ from a plain program's by a relative error of at most 0.019.
Values may be sent and summed in bfloat16 or wider, within the bound.
A program may use at most 128 MiB of HBM per device.

v0:
```python
import math

import jax
import jax.numpy as jnp
from jax import lax
from jax.sharding import PartitionSpec as P

HD = 128


def select_prompt(block, prompt, kv_heads):
    picked = lax.dynamic_index_in_dim(block, prompt, 0, keepdims=False)
    return picked.reshape(picked.shape[0], kv_heads, HD)


def stats_rows(query_part, grad_part, key_block, value_block, running_max, row_total, weighted):
    scores = jnp.einsum(
        "rkgd,pkd->kgrp", query_part, key_block, preferred_element_type=jnp.float32
    ) * (1.0 / math.sqrt(HD))
    dprob = jnp.einsum("rkgd,pkd->kgrp", grad_part, value_block, preferred_element_type=jnp.float32)
    new_max = jnp.max(scores, axis=-1)
    shrink = jnp.exp(running_max - new_max)
    exp_scores = jnp.exp(scores - new_max[..., None])
    row_total = row_total * shrink + jnp.sum(exp_scores, axis=-1)
    weighted = weighted * shrink + jnp.sum(exp_scores * dprob, axis=-1)
    return (new_max, row_total, weighted)


def grads_rows(query_part, grad_part, key_block, value_block, log_norm, row_delta):
    scaling = 1.0 / math.sqrt(HD)
    scores = (
        jnp.einsum("rkgd,pkd->kgrp", query_part, key_block, preferred_element_type=jnp.float32)
        * scaling
    )
    probs = jnp.exp(scores - log_norm[..., None])
    dprob = jnp.einsum("rkgd,pkd->kgrp", grad_part, value_block, preferred_element_type=jnp.float32)
    weights = probs.astype(jnp.bfloat16)
    dscore = (probs * (dprob - row_delta[..., None])).astype(jnp.bfloat16)
    query_term = jnp.einsum("kgrp,pkd->rkgd", dscore, key_block, preferred_element_type=jnp.float32)
    key_term = (
        jnp.einsum("kgrp,rkgd->pkd", dscore, query_part, preferred_element_type=jnp.float32)
        * scaling
    )
    value_term = jnp.einsum(
        "kgrp,rkgd->pkd", weights, grad_part, preferred_element_type=jnp.float32
    )
    return (query_term, key_term, value_term)


def shards(queries, out_grad, prompt_keys, prompt_values, resp_prompt, resp_len):
    row_count = queries.shape[0]
    kv_cols = prompt_keys.shape[2]
    kv_heads = kv_cols // HD
    group_size = queries.shape[1] // HD // kv_heads
    prompts = prompt_keys.shape[0]
    prompt = resp_prompt[0]
    length = resp_len[0]
    live_rows = jnp.arange(row_count, dtype=jnp.int32) < length
    query_heads = queries.reshape(row_count, kv_heads, group_size, HD)
    grad_live = jnp.where(live_rows[:, None], out_grad, jnp.zeros_like(out_grad))
    grad_heads = grad_live.reshape(row_count, kv_heads, group_size, HD)
    chosen = (jnp.arange(prompts, dtype=jnp.int32) == prompt).astype(jnp.float32)[:, None, None]

    def by_rows(compute):
        return compute(row_count)

    stat_shape = (kv_heads, group_size, row_count)
    start_stats = (
        jnp.full(stat_shape, -jnp.inf, jnp.float32),
        jnp.zeros(stat_shape, jnp.float32),
        jnp.zeros(stat_shape, jnp.float32),
    )
    pieces = (
        lax.all_gather(prompt_keys, "blk", axis=1, tiled=True),
        lax.all_gather(prompt_values, "blk", axis=1, tiled=True),
    )
    key_block = select_prompt(pieces[0], prompt, kv_heads)
    value_block = select_prompt(pieces[1], prompt, kv_heads)

    def compute(row_limit):
        fresh_stats = stats_rows(
            query_heads,
            grad_heads,
            key_block,
            value_block,
            start_stats[0],
            start_stats[1],
            start_stats[2],
        )
        return tuple(
            (
                jnp.concatenate([fresh_part, older[..., row_limit:]], axis=-1)
                for fresh_part, older in zip(fresh_stats, start_stats)
            )
        )

    running_max, row_total, weighted = by_rows(compute)
    counted = row_total > 0.0
    safe_total = jnp.where(counted, row_total, jnp.float32(1.0))
    log_norm = jnp.where(counted, running_max + jnp.log(safe_total), jnp.float32(0.0))
    row_delta = weighted / safe_total
    query_start = jnp.zeros((row_count, kv_heads, group_size, HD), jnp.float32)
    pieces = (
        lax.all_gather(prompt_keys, "blk", axis=1, tiled=True),
        lax.all_gather(prompt_values, "blk", axis=1, tiled=True),
    )
    grad_key_block = select_prompt(pieces[0], prompt, kv_heads)
    grad_value_block = select_prompt(pieces[1], prompt, kv_heads)
    query_acc = query_start

    def compute(row_limit):
        query_term, key_term, value_term = grads_rows(
            query_heads, grad_heads, grad_key_block, grad_value_block, log_norm, row_delta
        )
        query_new = jnp.concatenate([query_term, query_acc[row_limit:]], axis=0)
        return (query_new, key_term.reshape(-1, kv_cols), value_term.reshape(-1, kv_cols))

    query_acc, key_term, value_term = by_rows(compute)
    key_rows = key_term
    value_rows = value_term
    query_acc, key_rows, value_rows = (query_acc, key_rows, value_rows)
    key_grad, value_grad = (
        lax.psum_scatter(chosen * key_rows[None], ("blk", "resp"), scatter_dimension=1, tiled=True),
        lax.psum_scatter(
            chosen * value_rows[None], ("blk", "resp"), scatter_dimension=1, tiled=True
        ),
    )
    query_flat = (query_acc * (1.0 / math.sqrt(HD))).reshape(row_count, -1)
    query_grad = jnp.where(live_rows[:, None], query_flat, jnp.float32(0.0)).astype(jnp.bfloat16)
    return (query_grad, key_grad.astype(jnp.bfloat16), value_grad.astype(jnp.bfloat16))


def solution(mesh):
    placed = (
        P(("blk", "resp"), "head"),
        P(("blk", "resp"), "head"),
        P(None, "blk", "head"),
        P(None, "blk", "head"),
        P(("blk", "resp")),
        P(("blk", "resp")),
    )
    return jax.shard_map(
        shards,
        mesh=mesh,
        in_specs=placed,
        out_specs=(
            P(("blk", "resp"), "head"),
            P(None, ("blk", "resp"), "head"),
            P(None, ("blk", "resp"), "head"),
        ),
        check_vma=False,
    )
```

profile of v0, /device:TPU:1, one launch (start us, length us, event | category | flops | bytes accessed | tf_op | source)
XLA Modules:
  0.0 1557.1 jit_solution(12999579748202391523)
XLA Ops:
  7.2 0.0 all-gather.3.cloned.1.call-start
  7.2 1.5 copy.34
  8.7 0.0 all-gather.3.cloned.1.call-update
  8.8 0.0 all-gather.5.cloned.1.call-start
  8.8 1.5 copy.38
  10.4 0.0 all-gather.5.cloned.1.call-update
  11.0 1.5 copy.65
  13.2 1.4 select_bitcast_fusion
  14.6 0.2 copy.66
  14.8 1.3 dynamic-slice
  16.7 60.2 %all-gather.3.cloned.1.call-done = bf16[2,1024,256]{2,0,1:T(2,128)(2,1)} async-done(((bf16[2,64,256]{2,0,1:T(2,128)(2,1)}), bf16[2,1024,256]{2,0,1:T(2,128)(2,1)}) %all-gather.3.cloned.1.call-update) | async-done | bytes 1048592 | tf_op jit(solution)/shard_map/all_gather | solution.py:104
  77.0 70.6 %all-gather.5.cloned.1.call-done = bf16[2,1024,256]{2,0,1:T(2,128)(2,1)} async-done(((bf16[2,64,256]{2,0,1:T(2,128)(2,1)}), bf16[2,1024,256]{2,0,1:T(2,128)(2,1)}) %all-gather.5.cloned.1.call-update) | async-done | bytes 1048592 | tf_op jit(solution)/shard_map/all_gather | solution.py:105
  147.6 5.0 constant_dynamic-slice_fusion
  152.6 2.3 copy.63
  155.0 3.5 copy.64
  158.5 2.4 bitcast_reduce_fusion
  160.9 9.9 fusion.6
  170.8 0.8 compare_select_fusion
  171.5 13.3 fusion.5
  184.8 0.0 copy-start
  184.8 7.4 fusion.7
  192.2 0.0 copy-done
  192.2 2.3 convolution_multiply_fusion
  194.5 12.4 copy.47
  206.9 0.0 copy-start.2
  206.9 5.8 fusion.10
  212.7 0.0 copy-start.1
  212.7 2.6 copy.48
  215.3 0.0 copy-done.2
  215.3 1.3 copy.46
  216.6 3.3 broadcast_multiply_fusion
  220.0 1325.8 %all-reduce.4 = (bf16[2,1024,256]{2,1,0:T(8,128)(2,1)}, bf16[2,1024,256]{2,1,0:T(8,128)(2,1)}) all-reduce(f32[2,1024,256]{2,1,0:T(8,128)} %get-tuple-element.12, f32[2,1024,256]{2,1,0:T(8,128)S(1)} %get-tuple-element.11), channel_id=2, replica_groups=mesh['blk'=16,'resp'=16,'head'=2] {'blk','resp'}, use_global_device_ids=true, to_apply=%region_3.4.clone | all-reduce | flops 1048576 | bytes 6291456
  1545.8 1.3 dynamic-slice_convert_fusion
  1547.1 1.3 dynamic-slice_convert_fusion.1
  1548.4 0.0 copy-done.1
  1548.4 0.6 copy.43
  1549.1 1.2 select_convert_fusion
  (2 shorter events, 0.0 us)
Async XLA Ops:
  7.2 69.8 %all-gather.3.cloned.1.call-start = ((), (), s32[]{:S(2)}) async-start(), calls=%async_computation | async-start | bytes 1114112 | tf_op jit(solution)/shard_map/all_gather | solution.py:104
  8.8 138.8 %all-gather.5.cloned.1.call-start = ((), (), s32[]{:S(2)}) async-start(), calls=%async_computation.1 | async-start | bytes 1114112 | tf_op jit(solution)/shard_map/all_gather | solution.py:105
  184.8 7.4 copy-start
  206.9 8.5 copy-start.2
  212.7 1335.7 %copy-start.1 = (bf16[2,128,8,256]{3,1,2,0:T(8,128)(2,1)S(1)}, bf16[2,128,8,256]{3,1,2,0:T(8,128)(2,1)}, u32[]{:S(2)}) copy-start(bf16[2,128,8,256]{3,1,2,0:T(8,128)(2,1)} %convolution_multiply_fusion) | copy-start | bytes 3145732
Sparse Core Ops, SparseCore 0:
  10.1 66.8 all-gather.2
  79.6 67.9 all-gather.4
where the time goes:
time: 1560 us
  blocking collectives  1330 us (85%)
  waiting for transfers between devices  131 us (8%)
  local copies, waits for them, and re-layouts  36.5 us (2%)
  matrix products  27.7 us (2%)
  other arithmetic  20 us (1%)
  between operations  16.1 us (1%)
    unnamed x1, blocking collectives  1330 us
    all_gather x1, waiting for transfers between devices, shards(): lax.all_gather(prompt_values, 'blk', axis=1, tiled=True)  70.6 us
    all_gather x1, waiting for transfers between devices, shards(): lax.all_gather(prompt_keys, 'blk', axis=1, tiled=True)  60.2 us
  transfers between devices with their start and end apart: 2, of which 2 were waited for; matrix products, arithmetic and copies ran while one was open for 0% of the time, Pallas kernels for 0%

commit v1 on v0

v1 whole, which is shorter than its diff:
```python
import functools
import math

import jax
import jax.numpy as jnp
from jax import lax
from jax.experimental import pallas as pl
from jax.experimental.pallas import tpu as pltpu
from jax.sharding import PartitionSpec as P

HD = 128
MESH = pl.DeviceIdType.MESH
F32 = jnp.float32
BF16 = jnp.bfloat16
NX = 4
NY = 2
CT = 8
JUMP = 2


def gather_plan(blocks):
    up, down = blocks // 2, (blocks - 1) // 2
    steps, slots, gone = [], {0: 0}, 0
    while True:
        sends = [(-gone, d, -gone - d) for d in range(1, JUMP + 1) if gone + d <= up]
        sends += [(gone, -d, gone + d) for d in range(1, JUMP + 1) if gone + d <= down]
        if not sends:
            return steps, slots
        for _, _, offset in sends:
            slots[offset] = len(slots)
        steps.append(sends)
        gone += JUMP


def kernel(
    blocks,
    groups,
    q_hbm,
    g_hbm,
    k_in,
    v_in,
    prompt_ref,
    len_ref,
    dq_hbm,
    dk_out,
    dv_out,
    q_ref,
    g_ref,
    dq_ref,
    kv,
    kc,
    acc,
    core_out,
    core_in,
    x_out,
    x_in,
    x_own,
    y_out,
    y_in,
    z_out,
    z_in,
    last_out,
    last_in,
    flag,
    in_sem,
    out_sem,
    kv_send,
    kv_recv,
    share_send,
    share_recv,
    core_send,
    core_recv,
    x_send,
    x_recv,
    y_send,
    y_recv,
    z_send,
    z_recv,
    last_send,
    last_recv,
    flag_send,
    flag_recv,
):
    b, s = lax.axis_index("blk"), lax.axis_index("resp")
    y, x, c = s // (2 * NX), (s // 2) % NX, s % 2
    other_core = {"resp": s + 1 - 2 * c}
    other_y = {"resp": s + (1 - 2 * y) * (2 * NX)}
    steps, slots = gather_plan(blocks)

    def at_x(i):
        return {"resp": y * (2 * NX) + ((x + i) % NX) * 2 + c}

    def at_blk(offset):
        return {"blk": (b + offset + blocks) % blocks}

    def remote(src, dst, send, recv, to):
        return pltpu.make_async_remote_copy(
            src_ref=src, dst_ref=dst, send_sem=send, recv_sem=recv, device_id=to, device_id_type=MESH
        )

    load_q = pltpu.make_async_copy(q_hbm, q_ref, in_sem.at[0])
    load_g = pltpu.make_async_copy(g_hbm, g_ref, in_sem.at[1])
    load_q.start()
    load_g.start()

    partners = [other_core, other_y] + [at_x(i) for i in range(1, NX)]
    partners += [at_blk(o) for o in slots if o != 0]
    barrier = pltpu.get_barrier_semaphore()
    for to in partners:
        pl.semaphore_signal(barrier, inc=1, device_id=to, device_id_type=MESH)

    for kind, ref in enumerate((k_in, v_in)):
        for p in range(2):
            rows = ref[p].astype(F32)
            parts = [
                rows[(iy * NX + ix) * CT : (iy * NX + ix + 1) * CT]
                for ix in range(NX)
                for iy in range(NY)
            ]
            rows = jnp.concatenate(parts, axis=0).astype(BF16)
            for h in range(2):
                kv[kind, h, 0, p] = rows[:, h * HD : (h + 1) * HD]
    mine = prompt_ref[0].astype(F32)
    flag[0] = jnp.full((16, HD), 1.0, F32).astype(BF16) * mine.astype(BF16)
    pl.semaphore_wait(barrier, len(partners))

    flag_copy = remote(flag.at[0], flag.at[1], flag_send, flag_recv, other_core)
    flag_copy.start()

    def block_copy(h, step, i):
        held, jump, offset = steps[step][i]
        return remote(
            kv.at[c, h, slots[held]],
            kv.at[c, h, slots[offset]],
            kv_send.at[h, slots[offset]],
            kv_recv.at[h, slots[offset]],
            at_blk(jump),
        )

    def share_copy(h, step):
        first, count = slots[steps[step][0][2]], len(steps[step])
        part = kv.at[c, h, pl.ds(first, count)]
        return remote(part, part, share_send.at[h, step], share_recv.at[h, step], other_core)

    def gather_begin(h):
        for i in range(len(steps[0])):
            block_copy(h, 0, i).start()

    def gather_step(h, step):
        onward = set()
        if step + 1 < len(steps):
            onward = {held for held, _, _ in steps[step + 1]}
        for wanted in (True, False):
            for i, (_, _, offset) in enumerate(steps[step]):
                if (offset in onward) == wanted:
                    block_copy(h, step, i).wait_recv()
            if wanted and step + 1 < len(steps):
                for i in range(len(steps[step + 1])):
                    block_copy(h, step + 1, i).start()
        share_copy(h, step).start()

    def gather_end(h):
        for step in range(len(steps)):
            share_copy(h, step).wait_recv()

    gather_begin(0)
    gather_begin(1)
    for step in range(len(steps)):
        gather_step(0, step)
    gather_end(0)
    load_q.wait()
    load_g.wait()
    flag_copy.wait_recv()

    scaling = 1.0 / math.sqrt(HD)
    rate = scaling * math.log2(math.e)
    length = len_ref[0]
    rows_live = lax.broadcasted_iota(jnp.int32, (q_ref.shape[0], HD), 0) < length

    def dot(a, o, ca, co):
        return lax.dot_general(a, o, (((ca,), (co,)), ((), ())), preferred_element_type=F32)

    def begin_head(h):
        second = prompt_ref[0] == 1
        for kind in range(2):
            block = jnp.where(second, kv[kind, h, :, 1], kv[kind, h, :, 0])
            kc[kind] = block.reshape(kc.shape[1], HD)
        acc[h] = jnp.zeros_like(acc[h])

    def unit(u):
        cols = pl.ds(pl.multiple_of(u * HD, HD), HD)
        q = q_ref[:, cols]
        g = jnp.where(rows_live, g_ref[:, cols], jnp.zeros((), BF16))
        scores = dot(kc[0], q, 1, 1)
        dprob = dot(kc[1], g, 1, 1)
        top = jnp.max(scores, axis=0, keepdims=True)
        e = jnp.exp2((scores - top) * rate)
        total = jnp.sum(e, axis=0, keepdims=True)
        probs = e * (1.0 / total)
        delta = jnp.sum(probs * dprob, axis=0, keepdims=True)
        dscore = (probs * (dprob - delta)).astype(BF16)
        weights = probs.astype(BF16)
        h = u // groups
        acc[h, 0] += dot(dscore, q, 1, 0).reshape(acc.shape[2:])
        acc[h, 1] += dot(weights, g, 1, 0).reshape(acc.shape[2:])
        dq_ref[:, cols] = (dot(dscore, kc[0], 0, 0) * scaling).astype(BF16)

    def core_copy(h):
        return remote(core_out.at[h], core_in.at[h], core_send.at[h], core_recv.at[h], other_core)

    def x_copy(h, i):
        return remote(
            x_out.at[h, i], x_in.at[h, i], x_send.at[h, i], x_recv.at[h, i], at_x(i + 1)
        )

    def y_copy(h):
        return remote(y_out.at[h], y_in.at[h], y_send.at[h], y_recv.at[h], other_y)

    def z_copy(h, offset):
        at = slots[offset]
        return remote(
            z_out.at[h, at], z_in.at[h, at], z_send.at[h, at], z_recv.at[h, at], at_blk(offset)
        )

    def reduce_core(h):
        core_out[h] = (acc[h, 1 - c] * jnp.where(c == 0, 1.0, scaling)).astype(BF16)
        core_copy(h).start()

    def reduce_x(h):
        core_copy(h).wait_recv()
        theirs = flag[1, 0:1].astype(F32)
        own = [1.0 - mine, mine]
        other = [1.0 - theirs, theirs]
        factor = jnp.where(c == 0, scaling, 1.0)

        def chunk(at):
            a = acc[h, c, :, at] * factor
            o = core_in[h, :, at].astype(F32)
            both = [a * own[p] + o * other[p] for p in range(2)]
            return [
                jnp.concatenate([t[:, iy * CT : (iy + 1) * CT] for t in both], axis=1)
                for iy in range(NY)
            ]

        for i in range(1, NX):
            for iy, part in enumerate(chunk((x + i) % NX)):
                x_out[h, i - 1, iy] = part.astype(BF16)
            x_copy(h, i - 1).start()
        for iy, part in enumerate(chunk(x)):
            x_own[h, iy] = part

    def reduce_y(h):
        for i in range(NX - 1):
            x_copy(h, i).wait_recv()

        def total(at):
            t = x_own[h, at]
            for i in range(NX - 1):
                t += x_in[h, i, at].astype(F32)
            return t

        y_out[h] = total(1 - y).astype(BF16)
        y_copy(h).start()
        x_own[h, 0] = total(y)

    def reduce_z(h):
        y_copy(h).wait_recv()
        t = x_own[h, 0] + y_in[h].astype(F32)
        x_own[h, 0] = t
        z_out[h] = t.astype(BF16)
        for offset in slots:
            if offset != 0:
                z_copy(h, offset).start()

    def reduce_last(h):
        for offset in slots:
            if offset != 0:
                z_copy(h, offset).wait_recv()
        t = x_own[h, 0, 0]
        for at in range(1, blocks):
            t += z_in[h, at].astype(F32)
        last_out[h] = t.astype(BF16)

    def body(u, carry):
        @pl.when(u == groups)
        def _():
            gather_end(1)

        @pl.when(u % groups == 0)
        def _():
            begin_head(u // groups)

        unit(u)
        for step in range(len(steps)):

            @pl.when(u == step + 1)
            def _(step=step):
                gather_step(1, step)

        phases = (reduce_core, reduce_x, reduce_y, reduce_z, reduce_last)
        for n, phase in enumerate(phases):

            @pl.when(u == groups - 1 + min(2 * n, groups))
            def _(phase=phase):
                phase(0)

        return carry

    lax.fori_loop(0, 2 * groups, body, 0)
    store_q = pltpu.make_async_copy(dq_ref, dq_hbm, out_sem)
    store_q.start()
    reduce_core(1)
    reduce_x(1)
    reduce_y(1)
    reduce_z(1)
    reduce_last(1)

    final = remote(last_out, last_in, last_send, last_recv, other_core)
    final.start()
    final.wait_recv()
    half = CT // 2
    for kind, out in enumerate((dk_out, dv_out)):
        for h in range(2):
            tile = jnp.where(c == kind, last_out[h].astype(F32), last_in[h].astype(F32))
            for p in range(2):
                low = tile[p * CT : p * CT + half]
                high = tile[p * CT + half : (p + 1) * CT]
                out[p, :, h * HD : (h + 1) * HD] = jnp.where(c == 0, low, high).astype(BF16)

    flag_copy.wait_send()
    for h in range(2):
        for step in range(len(steps)):
            for i in range(len(steps[step])):
                block_copy(h, step, i).wait_send()
        for step in range(len(steps)):
            share_copy(h, step).wait_send()
        core_copy(h).wait_send()
        for i in range(NX - 1):
            x_copy(h, i).wait_send()
        y_copy(h).wait_send()
        for offset in slots:
            if offset != 0:
                z_copy(h, offset).wait_send()
    final.wait_send()
    store_q.wait()


def solution(mesh):
    blocks = mesh.shape["blk"]

    def shards(queries, out_grad, prompt_keys, prompt_values, resp_prompt, resp_len):
        rows, columns = queries.shape
        block_rows = prompt_keys.shape[1]
        groups = columns // HD // 2
        steps = len(gather_plan(blocks)[0])
        dma = pltpu.SemaphoreType.DMA
        return pl.pallas_call(
            functools.partial(kernel, blocks, groups),
            out_shape=(
                jax.ShapeDtypeStruct(queries.shape, BF16),
                jax.ShapeDtypeStruct((2, CT // 2, 2 * HD), BF16),
                jax.ShapeDtypeStruct((2, CT // 2, 2 * HD), BF16),
            ),
            in_specs=[
                pl.BlockSpec(memory_space=pl.ANY),
                pl.BlockSpec(memory_space=pl.ANY),
                pl.BlockSpec(memory_space=pltpu.VMEM),
                pl.BlockSpec(memory_space=pltpu.VMEM),
                pl.BlockSpec(memory_space=pltpu.SMEM),
                pl.BlockSpec(memory_space=pltpu.SMEM),
            ],
            out_specs=(
                pl.BlockSpec(memory_space=pl.ANY),
                pl.BlockSpec(memory_space=pltpu.VMEM),
                pl.BlockSpec(memory_space=pltpu.VMEM),
            ),
            scratch_shapes=[
                pltpu.VMEM((rows, columns), BF16),
                pltpu.VMEM((rows, columns), BF16),
                pltpu.VMEM((rows, columns), BF16),
                pltpu.VMEM((2, 2, blocks, 2, block_rows, HD), BF16),
                pltpu.VMEM((2, blocks * block_rows, HD), BF16),
                pltpu.VMEM((2, 2, blocks, NX, NY * CT, HD), F32),
                pltpu.VMEM((2, blocks, NX, NY * CT, HD), BF16),
                pltpu.VMEM((2, blocks, NX, NY * CT, HD), BF16),
                pltpu.VMEM((2, NX - 1, NY, blocks, 2 * CT, HD), BF16),
                pltpu.VMEM((2, NX - 1, NY, blocks, 2 * CT, HD), BF16),
                pltpu.VMEM((2, NY, blocks, 2 * CT, HD), F32),
                pltpu.VMEM((2, blocks, 2 * CT, HD), BF16),
                pltpu.VMEM((2, blocks, 2 * CT, HD), BF16),
                pltpu.VMEM((2, blocks, 2 * CT, HD), BF16),
                pltpu.VMEM((2, blocks, 2 * CT, HD), BF16),
                pltpu.VMEM((2, 2 * CT, HD), BF16),
                pltpu.VMEM((2, 2 * CT, HD), BF16),
                pltpu.VMEM((2, 16, HD), BF16),
                dma((2,)),
                dma,
                dma((2, blocks)),
                dma((2, blocks)),
                dma((2, steps)),
                dma((2, steps)),
                dma((2,)),
                dma((2,)),
                dma((2, NX - 1)),
                dma((2, NX - 1)),
                dma((2,)),
                dma((2,)),
                dma((2, blocks)),
                dma((2, blocks)),
                dma,
                dma,
                dma,
                dma,
            ],
            compiler_params=pltpu.CompilerParams(
                collective_id=0, has_side_effects=True, vmem_limit_bytes=56 << 20
            ),
        )(queries, out_grad, prompt_keys, prompt_values, resp_prompt, resp_len)

    rows = P(("blk", "resp"), "head")
    blocks_in = P(None, "blk", "head")
    each = P(("blk", "resp"))
    sums = P(None, ("blk", "resp"), "head")
    return jax.shard_map(
        shards,
        mesh=mesh,
        in_specs=(rows, rows, blocks_in, blocks_in, each, each),
        out_specs=(rows, sums, sums),
        check_vma=False,
    )
```

time: 1560 us -> 111 us (0.07)
  blocking collectives: 1330 us -> 0 us
  waiting for transfers between devices: 131 us -> 0 us
  Pallas kernels: 0 us -> 105 us
  local copies, waits for them, and re-layouts: 36.5 us -> 3.57 us
  matrix products: 27.7 us -> 0 us
  other arithmetic: 20 us -> 0 us
    unnamed x1 -> x0, blocking collectives: 1330 us -> none
    all_gather x2 -> x0, waiting for transfers between devices: 131 us -> none  [the longest x1 70.6 us: shards(): lax.all_gather(prompt_values, 'blk', axis=1, tiled=True)]
    pallas_call x0 -> x1, Pallas kernels: none -> 105 us  [shards(): pl.pallas_call(functools.partial(kernel, blocks, groups), out_shape=(jax....]
    dot_general x5 -> x0, matrix products: 27.7 us -> none  [the longest x1 9.86 us: grads_rows(): jnp.einsum('rkgd,pkd->kgrp', grad_part, value_block, preferred_element_ty...]
  transfers between devices with their start and end apart: 2 -> 0, of which waited for: 2 -> 0; matrix products, arithmetic and copies ran while one was open for 0% -> 0% of each run, Pallas kernels for 0% -> 0%
where the time goes in v1:
time: 111 us
  Pallas kernels  105 us (95%)
  local copies, waits for them, and re-layouts  3.57 us (3%)
  between operations  1.94 us (2%)
    pallas_call x1, Pallas kernels, shards(): pl.pallas_call(functools.partial(kernel, blocks, groups), out_shape=(jax....  105 us
    unnamed x7, local copies, waits for them, and re-layouts  3.57 us

profile of v1, /device:TPU:1, one launch (start us, length us, event | category | flops | bytes accessed | tf_op | source)
XLA Modules:
  0.0 110.7 jit_solution(14037815938376255319)
XLA Ops:
  1.9 105.1 %shard_map.85 = (bf16[256,2048]{1,0:T(8,128)(2,1)}, bf16[2,4,256]{2,1,0:T(4,128)(2,1)}, bf16[2,4,256]{2,1,0:T(4,128)(2,1)}) custom-call(bf16[256,2048]{1,0:T(8,128)(2,1)} %q_hbm.1, bf16[256,2048]{1,0:T(8,128)(2,1)} %g_hbm.1, bf16[2,64,256]{2,1,0:T(8,128)(2,1)} %k_in.1, bf16[2,64,256]{2,1,0:T(8,128)(2,1)} %v_in.1, s32[1]{0:T(128)S(6)} %copy.12.prompt_ref, ...), custom_call_target="tpu_custom_call" | custom-call | tf_op jit(solution)/shard_map/pallas_call | solution.py:357
  107.1 0.0 copy-start.1
  107.1 2.3 %copy.14 = bf16[256,2048]{1,0:T(8,128)(2,1)} copy(bf16[256,2048]{1,0:T(8,128)(2,1)} %get-tuple-element.6) | data formatting | bytes 2097152
  109.4 0.0 copy-done.1
  109.4 0.0 copy-start
  109.4 0.6 copy.15
  110.0 0.1 copy-done
  110.1 0.6 copy.16
Async XLA Ops:
  107.1 2.3 %copy-start.1 = (bf16[2,4,256]{2,1,0:T(4,128)(2,1)S(1)}, bf16[2,4,256]{2,1,0:T(4,128)(2,1)}, u32[]{:S(2)}) copy-start(bf16[2,4,256]{2,1,0:T(4,128)(2,1)} %get-tuple-element.7) | copy-start | bytes 12292
  109.4 0.7 copy-start

commit v2 on v1

v2 whole, which is shorter than its diff:
```python
import functools
import math

import jax
import jax.numpy as jnp
from jax import lax
from jax.experimental import pallas as pl
from jax.experimental.pallas import tpu as pltpu
from jax.sharding import PartitionSpec as P

HD = 128
MESH = pl.DeviceIdType.MESH
F32 = jnp.float32
BF16 = jnp.bfloat16
NX = 4
NY = 2
PLANE = NX * NY
CT = 8
TILE = NY * CT
UNITS = 2


def kernel(
    blocks,
    groups,
    q_hbm,
    g_hbm,
    k_hbm,
    v_hbm,
    prompt_hbm,
    len_hbm,
    dq_ref,
    dk_out,
    dv_out,
    k_in,
    v_in,
    q_ref,
    g_ref,
    prompt_ref,
    len_ref,
    order,
    kv,
    kc,
    acc,
    core_out,
    core_in,
    plane_out,
    plane_in,
    z_out,
    z_in,
    z_own,
    last_out,
    last_in,
    flag,
    in_sem,
    kvz_send,
    kvz_recv,
    kvp_send,
    kvp_recv,
    kvc_send,
    kvc_recv,
    core_send,
    core_recv,
    plane_send,
    plane_recv,
    z_send,
    z_recv,
    last_send,
    last_recv,
    flag_send,
    flag_recv,
):
    b, s = lax.axis_index("blk"), lax.axis_index("resp")
    y, x, c = s // (2 * NX), (s // 2) % NX, s % 2
    other_core = {"resp": s + 1 - 2 * c}

    def shifted(i):
        return (y + i) % NY, (x + i // NY) % NX

    def behind(i):
        return (y + i) % NY, (x + NX - i // NY) % NX

    def at_plane(i):
        py, px = shifted(i)
        return {"resp": (py * NX + px) * 2 + c}

    def at_blk(offset):
        return {"blk": (b + offset) % blocks}

    def remote(src, dst, send, recv, to):
        return pltpu.make_async_remote_copy(
            src_ref=src, dst_ref=dst, send_sem=send, recv_sem=recv, device_id=to, device_id_type=MESH
        )

    others = range(1, blocks)
    mates = range(1, PLANE)
    partners = [other_core] + [at_plane(i) for i in mates] + [at_blk(o) for o in others]
    barrier = pltpu.get_barrier_semaphore()
    for to in partners:
        pl.semaphore_signal(barrier, inc=1, device_id=to, device_id_type=MESH)

    loads = [
        pltpu.make_async_copy(k_hbm, k_in, in_sem.at[0]),
        pltpu.make_async_copy(v_hbm, v_in, in_sem.at[1]),
        pltpu.make_async_copy(prompt_hbm, prompt_ref, in_sem.at[2]),
        pltpu.make_async_copy(len_hbm, len_ref, in_sem.at[3]),
        pltpu.make_async_copy(q_hbm, q_ref, in_sem.at[4]),
        pltpu.make_async_copy(g_hbm, g_ref, in_sem.at[5]),
    ]
    for load in loads:
        load.start()

    loads[0].wait()
    loads[1].wait()
    rows = jnp.where(c == 0, k_in[y].astype(F32), v_in[y].astype(F32))
    for ix in range(NX):
        parts = [rows[(iy * NX + ix) * CT : (iy * NX + ix + 1) * CT] for iy in range(NY)]
        order[ix] = jnp.concatenate(parts, axis=0)
    tile = order[x].astype(BF16)
    for h in range(2):
        kv[c, h, y, x, 0] = tile[:, h * HD : (h + 1) * HD]
    loads[2].wait()
    mine = prompt_ref[0].astype(F32)
    flag[0] = jnp.full((16, HD), 1.0, F32).astype(BF16) * mine.astype(BF16)
    pl.semaphore_wait(barrier, len(partners))

    def kvz_copy(h, offset):
        sent = kv.at[c, h, y, x, 0]
        return remote(
            sent, kv.at[c, h, y, x, blocks - offset], kvz_send.at[h, offset], kvz_recv.at[h, offset], at_blk(offset)
        )

    def kvp_copy(h, i, wait=False):
        py, px = behind(i) if wait else (y, x)
        part = kv.at[c, h, py, px]
        return remote(kv.at[c, h, y, x], part, kvp_send.at[h, i], kvp_recv.at[h, i], at_plane(i))

    def kvc_copy(h):
        return remote(kv.at[c, h], kv.at[c, h], kvc_send.at[h], kvc_recv.at[h], other_core)

    def gather_blk(h):
        for offset in others:
            kvz_copy(h, offset).start()

    def gather_plane(h):
        for offset in others:
            kvz_copy(h, offset).wait_recv()
        for i in mates:
            kvp_copy(h, i).start()

    def gather_core(h):
        for i in mates:
            kvp_copy(h, i, True).wait_recv()
        kvc_copy(h).start()

    flag_copy = remote(flag.at[0], flag.at[1], flag_send, flag_recv, other_core)
    flag_copy.start()
    gather_blk(0)
    gather_blk(1)
    gather_plane(0)
    gather_plane(1)
    gather_core(0)
    for load in loads[3:]:
        load.wait()
    flag_copy.wait_recv()
    kvc_copy(0).wait_recv()

    scaling = 1.0 / math.sqrt(HD)
    rate = scaling * math.log2(math.e)
    rows_live = lax.broadcasted_iota(jnp.int32, (q_ref.shape[0], HD), 0) < len_ref[0]

    def dot(a, o, ca, co):
        return lax.dot_general(a, o, (((ca,), (co,)), ((), ())), preferred_element_type=F32)

    def begin_head(h):
        second = prompt_ref[0] == 1
        for kind in range(2):
            kc[kind] = jnp.where(second, kv[kind, h, 1], kv[kind, h, 0])
        acc[h] = jnp.zeros_like(acc[h])

    positions = NX * blocks * TILE

    def units(t):
        keys, values = kc[0].reshape(positions, HD), kc[1].reshape(positions, HD)
        h = t // (groups // UNITS)
        started = []
        for i in range(UNITS):
            cols = pl.ds(pl.multiple_of((t * UNITS + i) * HD, HD), HD)
            q = q_ref[:, cols]
            g = jnp.where(rows_live, g_ref[:, cols], jnp.zeros((), BF16))
            started.append((cols, q, g, dot(keys, q, 1, 1), dot(values, g, 1, 1)))
        key_sum = value_sum = 0.0
        for cols, q, g, scores, dprob in started:
            top = jnp.max(scores, axis=0, keepdims=True)
            e = jnp.exp2((scores - top) * rate)
            probs = e * (1.0 / jnp.sum(e, axis=0, keepdims=True))
            delta = jnp.sum(probs * dprob, axis=0, keepdims=True)
            dscore = (probs * (dprob - delta)).astype(BF16)
            weights = probs.astype(BF16)
            key_sum += dot(dscore, q, 1, 0)
            value_sum += dot(weights, g, 1, 0)
            dq_ref[:, cols] = (dot(dscore, keys, 0, 0) * scaling).astype(BF16)
        acc[h, 0] += key_sum.reshape(acc.shape[2:])
        acc[h, 1] += value_sum.reshape(acc.shape[2:])

    def core_copy(h):
        return remote(core_out.at[h], core_in.at[h], core_send.at[h], core_recv.at[h], other_core)

    def plane_copy(h, i):
        return remote(
            plane_out.at[h, i], plane_in.at[h, i], plane_send.at[h, i], plane_recv.at[h, i], at_plane(i)
        )

    def z_copy(h, at):
        return remote(z_out.at[h, at], z_in.at[h, at], z_send.at[h, at], z_recv.at[h, at], at_blk(at))

    def reduce_core(h):
        core_out[h] = (acc[h, 1 - c] * jnp.where(c == 0, 1.0, scaling)).astype(BF16)
        core_copy(h).start()

    def reduce_plane(h):
        core_copy(h).wait_recv()
        theirs = flag[1, 0:1].astype(F32)
        own = [1.0 - mine, mine]
        other = [1.0 - theirs, theirs]
        factor = jnp.where(c == 0, scaling, 1.0)
        for dx in (2, 1, 3, 0):
            at = (x + dx) % NX
            a = acc[h, c, at] * factor
            o = core_in[h, at].astype(F32)
            both = [a * own[p] + o * other[p] for p in range(2)]
            for iy in range(NY):
                part = jnp.concatenate([t[:, iy * CT : (iy + 1) * CT] for t in both], axis=1)
                plane_out[h, dx * NY + (iy + NY - y) % NY] = part.astype(BF16)
            for i in range(dx * NY, dx * NY + NY):
                if i:
                    plane_copy(h, i).start()

    def reduce_z(h):
        for i in mates:
            plane_copy(h, i).wait_recv()
        total = plane_out[h, 0].astype(F32)
        for i in mates:
            total += plane_in[h, i].astype(F32)
        z_out[h] = total.astype(BF16)
        z_own[h] = total[0]
        for at in others:
            z_copy(h, at).start()

    def reduce_last(h):
        for at in others:
            z_copy(h, at).wait_recv()
        total = z_own[h]
        for at in others:
            total += z_in[h, at].astype(F32)
        last_out[h] = total.astype(BF16)

    turns = groups // UNITS

    def body(t, carry):
        @pl.when(t == 0)
        def _():
            begin_head(0)

        @pl.when(t == turns)
        def _():
            kvc_copy(1).wait_recv()
            begin_head(1)

        units(t)

        @pl.when(t == turns - 2)
        def _():
            gather_core(1)

        @pl.when(t == turns - 1)
        def _():
            reduce_core(0)

        @pl.when(t == turns)
        def _():
            reduce_plane(0)

        return carry

    lax.fori_loop(0, 2 * turns, body, 0)
    reduce_core(1)
    reduce_z(0)
    reduce_plane(1)
    reduce_last(0)
    reduce_z(1)
    reduce_last(1)

    final = remote(last_out, last_in, last_send, last_recv, other_core)
    final.start()
    final.wait_recv()
    half = CT // 2
    for kind, out in enumerate((dk_out, dv_out)):
        for h in range(2):
            tile = jnp.where(c == kind, last_out[h].astype(F32), last_in[h].astype(F32))
            for p in range(2):
                low = tile[p * CT : p * CT + half]
                high = tile[p * CT + half : (p + 1) * CT]
                out[p, :, h * HD : (h + 1) * HD] = jnp.where(c == 0, low, high).astype(BF16)

    flag_copy.wait_send()
    for h in range(2):
        for offset in others:
            kvz_copy(h, offset).wait_send()
            z_copy(h, offset).wait_send()
        for i in mates:
            kvp_copy(h, i).wait_send()
            plane_copy(h, i).wait_send()
        kvc_copy(h).wait_send()
        core_copy(h).wait_send()
    final.wait_send()


def solution(mesh):
    blocks = mesh.shape["blk"]

    def shards(queries, out_grad, prompt_keys, prompt_values, resp_prompt, resp_len):
        rows, columns = queries.shape
        groups = columns // HD // 2
        dma = pltpu.SemaphoreType.DMA
        vmem, smem = pltpu.VMEM, pltpu.SMEM
        in_hbm = pl.BlockSpec(memory_space=pltpu.HBM)
        in_vmem = pl.BlockSpec(memory_space=pltpu.VMEM)
        return pl.pallas_call(
            functools.partial(kernel, blocks, groups),
            out_shape=(
                vmem(queries.shape, BF16),
                vmem((2, CT // 2, 2 * HD), BF16),
                vmem((2, CT // 2, 2 * HD), BF16),
            ),
            in_specs=[in_hbm] * 6,
            out_specs=(in_vmem, in_vmem, in_vmem),
            scratch_shapes=[
                vmem(prompt_keys.shape, BF16),
                vmem(prompt_values.shape, BF16),
                vmem((rows, columns), BF16),
                vmem((rows, columns), BF16),
                smem((1,), jnp.int32),
                smem((1,), jnp.int32),
                vmem((NX, TILE, 2 * HD), F32),
                vmem((2, 2, 2, NX, blocks, TILE, HD), BF16),
                vmem((2, NX, blocks, TILE, HD), BF16),
                vmem((2, 2, NX, blocks, TILE, HD), F32),
                vmem((2, NX, blocks, TILE, HD), BF16),
                vmem((2, NX, blocks, TILE, HD), BF16),
                vmem((2, PLANE, blocks, 2 * CT, HD), BF16),
                vmem((2, PLANE, blocks, 2 * CT, HD), BF16),
                vmem((2, blocks, 2 * CT, HD), BF16),
                vmem((2, blocks, 2 * CT, HD), BF16),
                vmem((2, 2 * CT, HD), F32),
                vmem((2, 2 * CT, HD), BF16),
                vmem((2, 2 * CT, HD), BF16),
                vmem((2, 16, HD), BF16),
                dma((6,)),
                dma((2, blocks)),
                dma((2, blocks)),
                dma((2, PLANE)),
                dma((2, PLANE)),
                dma((2,)),
                dma((2,)),
                dma((2,)),
                dma((2,)),
                dma((2, PLANE)),
                dma((2, PLANE)),
                dma((2, blocks)),
                dma((2, blocks)),
                dma,
                dma,
                dma,
                dma,
            ],
            compiler_params=pltpu.CompilerParams(
                collective_id=0, has_side_effects=True, vmem_limit_bytes=56 << 20
            ),
        )(queries, out_grad, prompt_keys, prompt_values, resp_prompt, resp_len)

    rows = P(("blk", "resp"), "head")
    blocks_in = P(None, "blk", "head")
    each = P(("blk", "resp"))
    sums = P(None, ("blk", "resp"), "head")
    return jax.shard_map(
        shards,
        mesh=mesh,
        in_specs=(rows, rows, blocks_in, blocks_in, each, each),
        out_specs=(rows, sums, sums),
        check_vma=False,
    )
```

time: 111 us -> 87 us (0.78)
  Pallas kernels: 105 us -> 82.8 us
  local copies, waits for them, and re-layouts: 3.57 us -> 2.16 us
    pallas_call x1, Pallas kernels: 105 us -> 82.8 us  [shards(): pl.pallas_call(functools.partial(kernel, blocks, groups), out_shape=(vmem...]
    unnamed x7 -> x3, local copies, waits for them, and re-layouts: 3.57 us -> 2.16 us
where the time goes in v2:
time: 87 us; the launch traced here: 86.9 us
  Pallas kernels  82.8 us (95%)
  local copies, waits for them, and re-layouts  2.16 us (2%)
  between operations  1.93 us (2%)
    pallas_call x1, Pallas kernels, shards(): pl.pallas_call(functools.partial(kernel, blocks, groups), out_shape=(vmem...  82.8 us
    unnamed x3, local copies, waits for them, and re-layouts  2.16 us

profile of v2, /device:TPU:1, one launch (start us, length us, event | category | flops | bytes accessed | tf_op | source)
XLA Modules:
  0.0 86.9 jit_solution(8920607083110059885)
XLA Ops:
  1.9 82.8 %shard_map.85 = (bf16[256,2048]{1,0:T(8,128)(2,1)S(1)}, bf16[2,4,256]{2,1,0:T(4,128)(2,1)S(1)}, bf16[2,4,256]{2,1,0:T(4,128)(2,1)S(1)}) custom-call(bf16[256,2048]{1,0:T(8,128)(2,1)} %q_hbm.1, bf16[256,2048]{1,0:T(8,128)(2,1)} %g_hbm.1, bf16[2,64,256]{2,1,0:T(8,128)(2,1)} %k_hbm.1, bf16[2,64,256]{2,1,0:T(8,128)(2,1)} %v_hbm.1, s32[1]{0:T(128)S(6)} %copy.15.prompt_hbm, ...), custom_call_target="tpu_custom_call" | custom-call | tf_op jit(solution)/shard_map/pallas_call | solution.py:329
  84.7 1.0 %copy.12 = bf16[256,2048]{1,0:T(8,128)(2,1)} copy(bf16[256,2048]{1,0:T(8,128)(2,1)S(1)} %get-tuple-element.3) | data formatting | bytes 2097152
  85.7 0.6 copy.13
  86.3 0.6 copy.14

commit v3 on v2

v3 whole, which is shorter than its diff:
```python
import functools
import math

import jax
import jax.numpy as jnp
from jax import lax
from jax.experimental import pallas as pl
from jax.experimental.pallas import tpu as pltpu
from jax.sharding import PartitionSpec as P

HD = 128
MESH = pl.DeviceIdType.MESH
F32 = jnp.float32
BF16 = jnp.bfloat16
NX = 4
NY = 2
PLANE = NX * NY
CT = 8
TILE = NY * CT
NEAR = 4
UNITS = 4


def kernel(
    blocks,
    groups,
    q_hbm,
    g_hbm,
    k_hbm,
    v_hbm,
    prompt_hbm,
    len_hbm,
    dq_ref,
    dk_out,
    dv_out,
    k_in,
    v_in,
    q_ref,
    g_ref,
    prompt_ref,
    len_ref,
    order,
    kv,
    kc,
    qg,
    terms,
    acc,
    core_out,
    core_in,
    plane_out,
    plane_in,
    z_out,
    z_in,
    z_own,
    last_out,
    last_in,
    flag,
    in_sem,
    kvz_send,
    kvz_recv,
    kvp_send,
    kvp_recv,
    kvc_send,
    kvc_recv,
    core_send,
    core_recv,
    plane_send,
    plane_recv,
    z_send,
    z_recv,
    last_send,
    last_recv,
    flag_send,
    flag_recv,
):
    rows = q_ref.shape[0]
    b, s = lax.axis_index("blk"), lax.axis_index("resp")
    y, x, c = s // (2 * NX), (s // 2) % NX, s % 2
    other_core = {"resp": s + 1 - 2 * c}

    def shifted(i):
        return (y + i) % NY, (x + i // NY) % NX

    def behind(i):
        return (y + i) % NY, (x + NX - i // NY) % NX

    def at_plane(i):
        py, px = shifted(i)
        return {"resp": (py * NX + px) * 2 + c}

    def at_blk(offset):
        return {"blk": (b + offset) % blocks}

    def remote(src, dst, send, recv, to):
        return pltpu.make_async_remote_copy(
            src_ref=src, dst_ref=dst, send_sem=send, recv_sem=recv, device_id=to, device_id_type=MESH
        )

    def each(indices, act):
        def step(i, carry):
            act(i)
            return carry

        lax.fori_loop(indices.start, indices.stop, step, 0)

    others = range(1, blocks)
    mates = range(1, PLANE)
    partners = [other_core] + [at_plane(i) for i in mates] + [at_blk(o) for o in others]
    barrier = pltpu.get_barrier_semaphore()
    for to in partners:
        pl.semaphore_signal(barrier, inc=1, device_id=to, device_id_type=MESH)

    loads = [
        pltpu.make_async_copy(k_hbm, k_in, in_sem.at[0]),
        pltpu.make_async_copy(v_hbm, v_in, in_sem.at[1]),
        pltpu.make_async_copy(prompt_hbm, prompt_ref, in_sem.at[2]),
        pltpu.make_async_copy(len_hbm, len_ref, in_sem.at[3]),
        pltpu.make_async_copy(q_hbm, q_ref, in_sem.at[4]),
        pltpu.make_async_copy(g_hbm, g_ref, in_sem.at[5]),
    ]
    for load in loads:
        load.start()

    loads[0].wait()
    loads[1].wait()
    block = jnp.where(c == 0, k_in[y].astype(F32), v_in[y].astype(F32))
    for ix in range(NX):
        parts = [block[(iy * NX + ix) * CT : (iy * NX + ix + 1) * CT] for iy in range(NY)]
        order[ix] = jnp.concatenate(parts, axis=0)
    tile = order[x].astype(BF16)
    for h in range(2):
        kv[c, h, y, x, NEAR] = tile[:, h * HD : (h + 1) * HD]
    loads[2].wait()
    mine = prompt_ref[0].astype(F32)
    flag[0] = jnp.full((16, HD), 1.0, F32).astype(BF16) * mine.astype(BF16)
    pl.semaphore_wait(barrier, len(partners))

    near = range(0, 2 * NEAR + 1)
    far = range(2 * NEAR + 1, blocks)
    halves = (near, far)

    def kvz_copy(h, offset):
        return remote(
            kv.at[c, h, y, x, NEAR],
            kv.at[c, h, y, x, (blocks + NEAR - offset) % blocks],
            kvz_send.at[h, offset],
            kvz_recv.at[h, offset],
            at_blk(offset),
        )

    def each_offset(half, act):
        if half is far:
            each(range(NEAR + 1, blocks - NEAR), act)
        else:
            each(range(1, NEAR + 1), act)
            each(range(blocks - NEAR, blocks), act)

    def part_of(half):
        return pl.ds(half.start, len(half))

    def kvp_copy(h, half, i, wait=False):
        py, px = behind(i) if wait else (y, x)
        part, n = part_of(half), halves.index(half)
        return remote(
            kv.at[c, h, y, x, part],
            kv.at[c, h, py, px, part],
            kvp_send.at[h, n, i],
            kvp_recv.at[h, n, i],
            at_plane(i),
        )

    def kvc_copy(h, half, i, kind):
        py, px = behind(i)
        part, n = kv.at[kind, h, py, px, part_of(half)], halves.index(half)
        return remote(part, part, kvc_send.at[h, n, i], kvc_recv.at[h, n, i], other_core)

    def gather_blk(h):
        for half in halves:
            each_offset(half, lambda offset: kvz_copy(h, offset).start())

    def gather_plane(h):
        for half in halves:
            each_offset(half, lambda offset: kvz_copy(h, offset).wait_recv())
            each(mates, lambda i: kvp_copy(h, half, i).start())
            kvc_copy(h, half, 0, c).start()

    def gather_core(h):
        for half in halves:

            def passed(i):
                kvp_copy(h, half, i, True).wait_recv()
                kvc_copy(h, half, i, c).start()

            each(mates, passed)

    def gather_end(h):
        for half in halves:
            each(range(PLANE), lambda i: kvc_copy(h, half, i, 1 - c).wait_recv())

    flag_copy = remote(flag.at[0], flag.at[1], flag_send, flag_recv, other_core)
    flag_copy.start()
    gather_blk(0)
    for load in loads[3:]:
        load.wait()
    rows_live = lax.broadcasted_iota(jnp.int32, (rows, HD), 0) < len_ref[0]

    def place(u, carry):
        h, at = u // groups, pl.ds(pl.multiple_of(u % groups * rows, rows), rows)
        cols = pl.ds(pl.multiple_of(u * HD, HD), HD)
        qg[h, 0, at] = q_ref[:, cols]
        qg[h, 1, at] = jnp.where(rows_live, g_ref[:, cols], jnp.zeros((), BF16))
        return carry

    lax.fori_loop(0, 2 * groups, place, 0)
    gather_plane(0)
    gather_blk(1)
    gather_core(0)
    gather_plane(1)
    flag_copy.wait_recv()
    gather_end(0)

    scaling = 1.0 / math.sqrt(HD)
    rate = scaling * math.log2(math.e)
    def dot(a, o, ca, co):
        return lax.dot_general(a, o, (((ca,), (co,)), ((), ())), preferred_element_type=F32)

    positions = NX * blocks * TILE

    def choose(h):
        second = prompt_ref[0] == 1
        for kind in range(2):
            kc[h, kind] = jnp.where(second, kv[kind, h, 1], kv[kind, h, 0])

    def softmax_units(h):
        def step(t, carry):
            keys, values = kc[h, 0].reshape(positions, HD), kc[h, 1].reshape(positions, HD)
            started = []
            for i in range(UNITS):
                at = pl.ds(pl.multiple_of((t * UNITS + i) * rows, rows), rows)
                scores = dot(keys, qg[h, 0, at], 1, 1)
                started.append((at, scores, dot(values, qg[h, 1, at], 1, 1)))
            for at, scores, dprob in started:
                top = jnp.max(scores, axis=0, keepdims=True)
                e = jnp.exp2((scores - top) * rate)
                probs = e * (1.0 / jnp.sum(e, axis=0, keepdims=True))
                delta = jnp.sum(probs * dprob, axis=0, keepdims=True)
                dscore = (probs * (dprob - delta)).astype(BF16)
                terms[h, 0, :, :, at] = dscore.reshape(NX, blocks * TILE, rows)
                terms[h, 1, :, :, at] = probs.astype(BF16).reshape(NX, blocks * TILE, rows)
            return carry

        lax.fori_loop(0, groups // UNITS, step, 0)

    def query_units(h):
        def step(t, carry):
            keys = kc[h, 0].reshape(positions, HD)
            for i in range(UNITS):
                u = t * UNITS + i
                at = pl.ds(pl.multiple_of(u * rows, rows), rows)
                cols = pl.ds(pl.multiple_of((h * groups + u) * HD, HD), HD)
                dscore = terms[h, 0, :, :, at].reshape(positions, rows)
                dq_ref[:, cols] = (dot(dscore, keys, 0, 0) * scaling).astype(BF16)
            return carry

        lax.fori_loop(0, groups // UNITS, step, 0)

    def chunk_at(n):
        return (x + NX - 1 - n) % NX

    def core_copy(h, n):
        at = chunk_at(n)
        return remote(
            core_out.at[h, at], core_in.at[h, at], core_send.at[h, n], core_recv.at[h, n], other_core
        )

    def plane_copy(h, half, i):
        part, n = part_of(half), halves.index(half)
        return remote(
            plane_out.at[h, i, part],
            plane_in.at[h, i, part],
            plane_send.at[h, n, i],
            plane_recv.at[h, n, i],
            at_plane(i),
        )

    def z_copy(h, at):
        return remote(z_out.at[h, at], z_in.at[h, at], z_send.at[h, at], z_recv.at[h, at], at_blk(at + blocks - NEAR))

    def reduce_chunk(h, n):
        at = chunk_at(n)
        out = dot(terms[h, 1 - c, at], qg[h, 1 - c], 1, 0) * jnp.where(c == 0, 1.0, scaling)
        core_out[h, at] = out.astype(BF16).reshape(core_out.shape[2:])
        core_copy(h, n).start()
        own = dot(terms[h, c, at], qg[h, c], 1, 0) * jnp.where(c == 0, scaling, 1.0)
        acc[h, at] = own.reshape(acc.shape[2:])

    def reduce_plane(h, n):
        core_copy(h, n).wait_recv()
        theirs = flag[1, 0:1].astype(F32)
        own = [1.0 - mine, mine]
        other = [1.0 - theirs, theirs]
        dx, at = NX - 1 - n, chunk_at(n)
        a, o = acc[h, at], core_in[h, at].astype(F32)
        both = [a * own[p] + o * other[p] for p in range(2)]
        for iy in range(NY):
            part = jnp.concatenate([t[:, iy * CT : (iy + 1) * CT] for t in both], axis=1)
            plane_out[h, dx * NY + (iy + NY - y) % NY] = part.astype(BF16)
        plane_copy(h, far, dx * NY + 1).start()

        @pl.when(dx > 0)
        def _():
            plane_copy(h, far, dx * NY).start()

    def reduce_begin(h):
        def step(n):
            @pl.when(n < NX)
            def _():
                reduce_chunk(h, n)

            @pl.when(n > 0)
            def _():
                reduce_plane(h, n - 1)

        each(range(NX + 1), step)
        each(mates, lambda i: plane_copy(h, near, i).start())

    def each_other(half, act):
        if half is far:
            each(far, act)
        else:
            each(range(NEAR), act)
            each(range(NEAR + 1, 2 * NEAR + 1), act)

    def reduce_z(h):
        for half in (far, near):
            part = part_of(half)
            z_own[h, part] = plane_out[h, 0, part].astype(F32)

            def arrived(i):
                plane_copy(h, half, i).wait_recv()
                z_own[h, part] += plane_in[h, i, part].astype(F32)

            each(mates, arrived)
            z_out[h, part] = z_own[h, part].astype(BF16)
            each_other(half, lambda at: z_copy(h, at).start())

    def reduce_last(h):
        def arrived(at):
            z_copy(h, at).wait_recv()
            z_own[h, NEAR] += z_in[h, at].astype(F32)

        each_other(near, arrived)
        each_other(far, arrived)
        last_out[h] = z_own[h, NEAR].astype(BF16)

    def first_half(h):
        @pl.when(h == 1)
        def _():
            gather_core(1)
            gather_end(1)

        choose(h)
        softmax_units(h)
        reduce_begin(h)

    def second_half(h):
        reduce_z(h)
        query_units(h)

    each(range(2), first_half)
    each(range(2), second_half)
    def drain(h):
        each(others, lambda offset: kvz_copy(h, offset).wait_send())
        for half in halves:
            each_other(half, lambda at: z_copy(h, at).wait_send())

            def over_plane(i):
                kvp_copy(h, half, i).wait_send()
                plane_copy(h, half, i).wait_send()

            each(mates, over_plane)
            each(range(PLANE), lambda i: kvc_copy(h, half, i, c).wait_send())
        each(range(NX), lambda n: core_copy(h, n).wait_send())

    each(range(2), drain)
    flag_copy.wait_send()
    each(range(2), reduce_last)

    final = remote(last_out, last_in, last_send, last_recv, other_core)
    final.start()
    final.wait_recv()
    half = CT // 2
    for kind, out in enumerate((dk_out, dv_out)):
        for h in range(2):
            tile = jnp.where(c == kind, last_out[h].astype(F32), last_in[h].astype(F32))
            for p in range(2):
                low = tile[p * CT : p * CT + half]
                high = tile[p * CT + half : (p + 1) * CT]
                out[p, :, h * HD : (h + 1) * HD] = jnp.where(c == 0, low, high).astype(BF16)

    final.wait_send()


def solution(mesh):
    blocks = mesh.shape["blk"]

    def shards(queries, out_grad, prompt_keys, prompt_values, resp_prompt, resp_len):
        rows, columns = queries.shape
        groups = columns // HD // 2
        dma = pltpu.SemaphoreType.DMA
        vmem, smem = pltpu.VMEM, pltpu.SMEM
        in_hbm = pl.BlockSpec(memory_space=pltpu.HBM)
        in_vmem = pl.BlockSpec(memory_space=pltpu.VMEM)
        return pl.pallas_call(
            functools.partial(kernel, blocks, groups),
            out_shape=(
                vmem(queries.shape, BF16),
                vmem((2, CT // 2, 2 * HD), BF16),
                vmem((2, CT // 2, 2 * HD), BF16),
            ),
            in_specs=[in_hbm] * 6,
            out_specs=(in_vmem, in_vmem, in_vmem),
            scratch_shapes=[
                vmem(prompt_keys.shape, BF16),
                vmem(prompt_values.shape, BF16),
                vmem((rows, columns), BF16),
                vmem((rows, columns), BF16),
                smem((1,), jnp.int32),
                smem((1,), jnp.int32),
                vmem((NX, TILE, 2 * HD), F32),
                vmem((2, 2, 2, NX, blocks, TILE, HD), BF16),
                vmem((2, 2, NX, blocks, TILE, HD), BF16),
                vmem((2, 2, groups * rows, HD), BF16),
                vmem((2, 2, NX, blocks * TILE, groups * rows), BF16),
                vmem((2, NX, blocks, TILE, HD), F32),
                vmem((2, NX, blocks, TILE, HD), BF16),
                vmem((2, NX, blocks, TILE, HD), BF16),
                vmem((2, PLANE, blocks, 2 * CT, HD), BF16),
                vmem((2, PLANE, blocks, 2 * CT, HD), BF16),
                vmem((2, blocks, 2 * CT, HD), BF16),
                vmem((2, blocks, 2 * CT, HD), BF16),
                vmem((2, blocks, 2 * CT, HD), F32),
                vmem((2, 2 * CT, HD), BF16),
                vmem((2, 2 * CT, HD), BF16),
                vmem((2, 16, HD), BF16),
                dma((6,)),
                dma((2, blocks)),
                dma((2, blocks)),
                dma((2, 2, PLANE)),
                dma((2, 2, PLANE)),
                dma((2, 2, PLANE)),
                dma((2, 2, PLANE)),
                dma((2, NX)),
                dma((2, NX)),
                dma((2, 2, PLANE)),
                dma((2, 2, PLANE)),
                dma((2, blocks)),
                dma((2, blocks)),
                dma,
                dma,
                dma,
                dma,
            ],
            compiler_params=pltpu.CompilerParams(
                collective_id=0, has_side_effects=True, vmem_limit_bytes=56 << 20
            ),
        )(queries, out_grad, prompt_keys, prompt_values, resp_prompt, resp_len)

    rows = P(("blk", "resp"), "head")
    blocks_in = P(None, "blk", "head")
    each = P(("blk", "resp"))
    sums = P(None, ("blk", "resp"), "head")
    return jax.shard_map(
        shards,
        mesh=mesh,
        in_specs=(rows, rows, blocks_in, blocks_in, each, each),
        out_specs=(rows, sums, sums),
        check_vma=False,
    )
```

time: 87 us -> 77.9 us (0.90)
  Pallas kernels: 82.8 us -> 73.7 us
    pallas_call x1, Pallas kernels: 82.8 us -> 73.7 us  [shards(): pl.pallas_call(functools.partial(kernel, blocks, groups), out_shape=(vmem...]
where the time goes in v3:
time: 77.9 us; the launch traced here: 77.8 us
  Pallas kernels  73.7 us (95%)
  local copies, waits for them, and re-layouts  2.16 us (3%)
  between operations  1.93 us (2%)
    pallas_call x1, Pallas kernels, shards(): pl.pallas_call(functools.partial(kernel, blocks, groups), out_shape=(vmem...  73.7 us
    unnamed x3, local copies, waits for them, and re-layouts  2.16 us

profile of v3, /device:TPU:1, one launch (start us, length us, event | category | flops | bytes accessed | tf_op | source)
XLA Modules:
  0.0 77.8 jit_solution(10213798277481336557)
XLA Ops:
  1.9 73.7 %shard_map.85 = (bf16[256,2048]{1,0:T(8,128)(2,1)S(1)}, bf16[2,4,256]{2,1,0:T(4,128)(2,1)S(1)}, bf16[2,4,256]{2,1,0:T(4,128)(2,1)S(1)}) custom-call(bf16[256,2048]{1,0:T(8,128)(2,1)} %q_hbm.1, bf16[256,2048]{1,0:T(8,128)(2,1)} %g_hbm.1, bf16[2,64,256]{2,1,0:T(8,128)(2,1)} %k_hbm.1, bf16[2,64,256]{2,1,0:T(8,128)(2,1)} %v_hbm.1, s32[1]{0:T(128)S(6)} %copy.15.prompt_hbm, ...), custom_call_target="tpu_custom_call" | custom-call | tf_op jit(solution)/shard_map/pallas_call | solution.py:414
  75.6 1.0 %copy.12 = bf16[256,2048]{1,0:T(8,128)(2,1)} copy(bf16[256,2048]{1,0:T(8,128)(2,1)S(1)} %get-tuple-element.3) | data formatting | bytes 2097152
  76.6 0.6 copy.13
  77.2 0.6 copy.14

commit v4 on v3

--- a/solution.py
+++ b/solution.py
@@ -18,7 +18,8 @@
 CT = 8
 TILE = NY * CT
 NEAR = 4
-UNITS = 4
+UNITS = 8
+QUERY_UNITS = 4
 
 
 def kernel(
@@ -254,15 +255,15 @@
     def query_units(h):
         def step(t, carry):
             keys = kc[h, 0].reshape(positions, HD)
-            for i in range(UNITS):
-                u = t * UNITS + i
+            for i in range(QUERY_UNITS):
+                u = t * QUERY_UNITS + i
                 at = pl.ds(pl.multiple_of(u * rows, rows), rows)
                 cols = pl.ds(pl.multiple_of((h * groups + u) * HD, HD), HD)
                 dscore = terms[h, 0, :, :, at].reshape(positions, rows)
                 dq_ref[:, cols] = (dot(dscore, keys, 0, 0) * scaling).astype(BF16)
             return carry
 
-        lax.fori_loop(0, groups // UNITS, step, 0)
+        lax.fori_loop(0, groups // QUERY_UNITS, step, 0)
 
     def chunk_at(n):
         return (x + NX - 1 - n) % NX
@@ -401,6 +402,15 @@
     final.wait_send()
 
 
+def store_kernel(dq_ref, dk_ref, dv_ref, dq_hbm, dk_hbm, dv_hbm, sem):
+    pairs = ((dq_ref, dq_hbm), (dk_ref, dk_hbm), (dv_ref, dv_hbm))
+    copies = [pltpu.make_async_copy(src, dst, sem.at[n]) for n, (src, dst) in enumerate(pairs)]
+    for copy in copies:
+        copy.start()
+    for copy in copies:
+        copy.wait()
+
+
 def solution(mesh):
     blocks = mesh.shape["blk"]
 
@@ -411,7 +421,7 @@
         vmem, smem = pltpu.VMEM, pltpu.SMEM
         in_hbm = pl.BlockSpec(memory_space=pltpu.HBM)
         in_vmem = pl.BlockSpec(memory_space=pltpu.VMEM)
-        return pl.pallas_call(
+        grads = pl.pallas_call(
             functools.partial(kernel, blocks, groups),
             out_shape=(
                 vmem(queries.shape, BF16),
@@ -465,6 +475,14 @@
                 collective_id=0, has_side_effects=True, vmem_limit_bytes=56 << 20
             ),
         )(queries, out_grad, prompt_keys, prompt_values, resp_prompt, resp_len)
+        grads = [pltpu.with_memory_space_constraint(grad, pltpu.VMEM) for grad in grads]
+        return pl.pallas_call(
+            store_kernel,
+            out_shape=tuple(pltpu.HBM(grad.shape, BF16) for grad in grads),
+            in_specs=[in_vmem] * 3,
+            out_specs=(pl.BlockSpec(memory_space=pltpu.HBM),) * 3,
+            scratch_shapes=[dma((3,))],
+        )(*grads)
 
     rows = P(("blk", "resp"), "head")
     blocks_in = P(None, "blk", "head")

time: 77.9 us -> 76.1 us (0.977)
  local copies, waits for them, and re-layouts: 2.16 us -> 0 us
    unnamed x3 -> x0, local copies, waits for them, and re-layouts: 2.16 us -> none
    pallas_call x0 -> x1, Pallas kernels: none -> 1 us  [shards(): pl.pallas_call(store_kernel, out_shape=tuple((pltpu.HBM(grad.shape, BF16)...]
where the time goes in v4:
time: 76.1 us; the launch traced here: 75.9 us
  Pallas kernels  74 us (97%)
  between operations  1.93 us (3%)
    pallas_call x1, Pallas kernels, shards(): pl.pallas_call(functools.partial(kernel, blocks, groups), out_shape=(vmem...  73 us

profile of v4, /device:TPU:1, one launch (start us, length us, event | category | flops | bytes accessed | tf_op | source)
XLA Modules:
  0.0 75.9 jit_solution(13650240477710217008)
XLA Ops:
  1.9 73.0 %shard_map.85 = (bf16[256,2048]{1,0:T(8,128)(2,1)S(1)}, bf16[2,4,256]{2,1,0:T(4,128)(2,1)S(1)}, bf16[2,4,256]{2,1,0:T(4,128)(2,1)S(1)}) custom-call(bf16[256,2048]{1,0:T(8,128)(2,1)} %q_hbm.1, bf16[256,2048]{1,0:T(8,128)(2,1)} %g_hbm.1, bf16[2,64,256]{2,1,0:T(8,128)(2,1)} %k_hbm.1, bf16[2,64,256]{2,1,0:T(8,128)(2,1)} %v_hbm.1, s32[1]{0:T(128)S(6)} %copy.9.prompt_hbm, ...), custom_call_target="tpu_custom_call" | custom-call | tf_op jit(solution)/shard_map/pallas_call | solution.py:424
  74.9 1.0 %shard_map.86 = (bf16[256,2048]{1,0:T(8,128)(2,1)}, bf16[2,4,256]{2,1,0:T(4,128)(2,1)}, bf16[2,4,256]{2,1,0:T(4,128)(2,1)}) custom-call(bf16[256,2048]{1,0:T(8,128)(2,1)S(1)} %get-tuple-element.6.dq_ref, bf16[2,4,256]{2,1,0:T(4,128)(2,1)S(1)} %get-tuple-element.7.dk_ref, bf16[2,4,256]{2,1,0:T(4,128)(2,1)S(1)} %get-tuple-element.8.dv_ref), custom_call_target="tpu_custom_call" | custom-call | tf_op jit(solution)/shard_map/pallas_call | solution.py:479
